TPU v7x, 32 devices: a whole 2x2x4 slice. The times are simulated.
32 devices in a mesh: ga: 2 (over x), col: 16 (over z, y, core).
Axes of the slice: x: 2, y: 2, z: 4, core: 2. Of those that a mesh axis runs over, the one named last changes fastest.
Arguments:
- cholesky: bfloat16 [1024, 1024, 512], P(('ga', 'col')), parts along dimension 0, may hold values from -0.1875 to 0.1875
- amplitudes: bfloat16 [512, 512, 512], P('ga', 'col'), parts along dimension 0, may hold values from -0.25 to 0.25
Outputs:
- ladder: float32 [512, 2, 512], P('ga', None, 'col'), parts along dimension 0
There are 2 independent parts, one for each index of `ga`. A program takes and returns all parts, laid end to end along the dimension named above; each array names one. Nothing has to cross between parts.
All inputs are finite; a program needn't handle non-finite values.
Results may differ from a plain program's by a relative error of at most 0.0029.
Values may be sent and summed in bfloat16 or wider, within the bound.
A program may use at most 128 MiB of HBM per device.

v0:
```python
import jax
import jax.numpy as jnp
from jax import lax
from jax.sharding import PartitionSpec as P

A_WIN = 2


def shards(cholesky, amplitudes):
    window_local = jnp.transpose(cholesky[:, :, :A_WIN], (0, 2, 1))
    gathered = lax.all_gather(window_local, "col", axis=0, tiled=True)
    integrals = jnp.einsum(
        "clb,dal->acbd", cholesky, gathered, preferred_element_type=jnp.float32
    ).astype(jnp.bfloat16)
    partial_value = jnp.einsum(
        "pcd,acbd->pab", amplitudes, integrals, preferred_element_type=jnp.float32
    )
    return lax.psum_scatter(partial_value, "col", scatter_dimension=2, tiled=True)


def solution(mesh):
    in_specs = (P(("ga", "col"), None, None), P("ga", "col", None))
    out_specs = P("ga", None, "col")
    return jax.shard_map(shards, mesh=mesh, in_specs=in_specs, out_specs=out_specs, check_vma=False)
```

profile of v0, /device:TPU:0, one launch (start us, length us, event | category | flops | bytes accessed | tf_op | source)
XLA Modules:
  0.0 194.3 jit_solution(14769614902014618479)
XLA Ops:
  6.5 0.0 all-gather.2.cloned.1.call-start
  6.5 7.5 %slice.3 = bf16[32,1024,2]{2,1,0:T(8,128)(2,1)} slice(bf16[32,1024,512]{2,1,0:T(8,128)(2,1)} %param.2), slice={[0:32], [0:1024], [0:2]} | slice | bytes 262144 | tf_op jit(solution)/shard_map/slice | solution.py:10
  14.0 7.0 %copy.8 = bf16[32,1024,2]{1,2,0:T(2,128)(2,1)} copy(bf16[32,1024,2]{2,1,0:T(8,128)(2,1)} %slice.3) | data formatting | bytes 262144
  21.0 0.0 all-gather.2.cloned.1.call-update
  21.0 0.0 reduce-scatter.2.cloned.1.call-start
  21.1 44.2 %all-gather.2.cloned.1.call-done = bf16[512,2,1024]{2,1,0:T(2,128)(2,1)} async-done(((bf16[32,2,1024]{2,1,0:T(2,128)(2,1)}), bf16[512,2,1024]{2,1,0:T(2,128)(2,1)}) %all-gather.2.cloned.1.call-update) | async-done | bytes 2097168 | tf_op jit(solution)/shard_map/all_gather | solution.py:11
  65.3 43.2 %fusion.31 = bf16[2,32,512,512]{3,2,1,0:T(8,128)(2,1)} fusion(bf16[32,1024,512]{2,1,0:T(8,128)(2,1)} %param.2, bf16[512,2,1024,1]{2,1,0,3:T(2,128)(2,1)} %bitcast.36), kind=kOutput, calls=%fused_computation.1.clone.clone.clone.1 | convolution fusion | flops 34376515584 | bytes 69206016 | tf_op jit(solution)/shard_map/clb,dal->acbd/dot_general | solution.py:12
  108.4 22.7 %fusion.13 = f32[256,2,512]{0,2,1:T(8,128)} fusion(bf16[256,32,512]{2,1,0:T(8,128)(2,1)} %param.3, bf16[2,32,512,512]{3,2,1,0:T(8,128)(2,1)} %fusion.31), kind=kOutput, calls=%fused_computation.8 | convolution fusion | flops 8589934592 | bytes 42991616 | tf_op jit(solution)/shard_map/pcd,acbd->pab/dot_general | solution.py:15
  131.1 0.0 reduce-scatter.2.cloned.1.call-update
  131.2 56.3 %reduce-scatter.2.cloned.1.call-done = f32[256,2,32]{0,2,1:T(8,128)} async-done(((f32[256,2,512]{0,2,1:T(8,128)}), f32[256,2,32]{0,2,1:T(8,128)}) %reduce-scatter.2.cloned.1.call-update) | async-done | bytes 65552 | tf_op jit(solution)/shard_map/reduce_scatter | solution.py:18
Async XLA Ops:
  6.5 58.8 %all-gather.2.cloned.1.call-start = ((), (), s32[]{:S(2)}) async-start(), calls=%async_computation.1 | async-start | bytes 2228224 | tf_op jit(solution)/shard_map/all_gather | solution.py:11
  21.0 166.4 %reduce-scatter.2.cloned.1.call-start = ((), (), s32[]{:S(2)}) async-start(), calls=%async_computation.2 | async-start | bytes 1114112 | tf_op jit(solution)/shard_map/reduce_scatter | solution.py:18
Sparse Core Ops, SparseCore 0:
  21.2 44.0 all-gather.1
  131.3 56.1 reduce-scatter.1
where the time goes:
time: 195 us; the launch traced here: 194 us
  waiting for transfers between devices  101 us (52%)
  matrix products  65.8 us (34%)
  local copies, waits for them, and re-layouts  14.5 us (7%)
  between operations  13.4 us (7%)
    reduce_scatter x1, waiting for transfers between devices, shards(): lax.psum_scatter(partial_value, 'col', scatter_dimension=2, tiled=True)  56.3 us
    all_gather x1, waiting for transfers between devices, shards(): gathered = lax.all_gather(window_local, 'col', axis=0, tiled=True)  44.2 us
    dot_general x1, matrix products, shards(): jnp.einsum('clb,dal->acbd', cholesky, gathered, preferred_element_type=jn...  43.2 us
    dot_general x1, matrix products, shards(): jnp.einsum('pcd,acbd->pab', amplitudes, integrals, preferred_element_type...  22.7 us
    slice x1, local copies, waits for them, and re-layouts, shards(): window_local = jnp.transpose(cholesky[:, :, :A_WIN], (0, 2, 1))  7.51 us
    unnamed x1, local copies, waits for them, and re-layouts  6.97 us
  transfers between devices with their start and end apart: 2, of which 2 were waited for; matrix products, arithmetic and copies ran while one was open for 0% of the time, Pallas kernels for 0%

commit v1 on v0

v1 whole, which is shorter than its diff:
```python
import functools

import jax
import jax.numpy as jnp
from jax import lax
from jax.experimental import pallas as pl
from jax.experimental.pallas import tpu as pltpu
from jax.sharding import PartitionSpec as P

A_WIN = 2
PHASES = 2
F32 = jnp.float32
BF16 = jnp.bfloat16
MESH = pl.DeviceIdType.MESH


def kernel(n, lc, group, pc, chol, amps, out, bv, tt, traw, tf, sel, w, wa, xbuf, acc, acct,
           recv_a, summed, recv_b, lane_sem, rest_sem, t_sem, g_send, g_recv, f_send, f_recv,
           a_send, a_recv, b_send, b_recv):
    c_loc, nchol, v = chol.shape
    p_size = amps.shape[0]
    q_num = nchol // lc
    k_num = n // 2
    vb = v // n
    ph_rows = p_size // PHASES
    me = lax.axis_index("col")
    chip = me // 2
    core = lax.rem(me, 2)
    sib = chip * 2 + 1 - core

    def peer_at(i):
        return lax.rem(chip + i, k_num) * 2 + core

    def source_at(i):
        return lax.rem(chip - i + k_num, k_num) * 2 + core

    def lane_copy(q):
        rows = pl.ds(q * lc, lc)
        return pltpu.make_async_copy(chol.at[:, rows, pl.ds(0, 128)], bv.at[:, rows, pl.ds(0, 128)], lane_sem.at[q])

    def rest_copy(q):
        rows = pl.ds(q * lc, lc)
        return pltpu.make_async_copy(chol.at[:, rows, pl.ds(128, v - 128)], bv.at[:, rows, pl.ds(128, v - 128)], rest_sem.at[q])

    t_num = p_size // pc

    def t_copy(i):
        return pltpu.make_async_copy(amps.at[pl.ds(i * pc, pc)], traw.at[i % 2], t_sem.at[i % 2])

    for q in range(q_num):
        lane_copy(q).start()
    t_copy(0).start()
    t_copy(1).start()
    for q in range(q_num):
        rest_copy(q).start()

    barrier = pltpu.get_barrier_semaphore()
    pl.semaphore_signal(barrier, inc=1, device_id={"col": sib}, device_id_type=MESH)
    for i in range(1, k_num):
        pl.semaphore_signal(barrier, inc=1, device_id={"col": peer_at(i)}, device_id_type=MESH)

    lane = lax.broadcasted_iota(jnp.int32, (128, 128), 0)
    column = lax.broadcasted_iota(jnp.int32, (128, 128), 1)

    def make_sel(c, _):
        sel[c] = jnp.where((lane < A_WIN) & (column == lane * c_loc + c), 1.0, 0.0).astype(BF16)
        return 0

    lax.fori_loop(0, c_loc, make_sel, 0)
    pl.semaphore_wait(barrier, k_num)

    def remote(src, dst, send, recv, to):
        return pltpu.make_async_remote_copy(
            src_ref=src, dst_ref=dst, send_sem=send, recv_sem=recv, device_id={"col": to}, device_id_type=MESH)

    def gather_copy(q, i):
        to = sib if i == 0 else peer_at(i)
        return remote(w.at[q, me], w.at[q, me], g_send.at[q, i], g_recv.at[q, i], to)

    def forward_copy(q, i):
        block = w.at[q, source_at(i)]
        return remote(block, block, f_send.at[q, i], f_recv.at[q, i], sib)

    def extract(q):
        lane_copy(q).wait()

        def step(c, z):
            return z + jnp.dot(bv[c, pl.ds(q * lc, lc), pl.ds(0, 128)], sel[c], preferred_element_type=F32)

        z = lax.fori_loop(0, c_loc, step, jnp.zeros((lc, 128), F32), unroll=4)
        w[q, me] = jnp.transpose(z)[: A_WIN * c_loc].astype(BF16)
        for i in range(k_num):
            gather_copy(q, i).start()

    def forward(q):
        for i in range(1, k_num):
            gather_copy(q, i).wait_recv()
            forward_copy(q, i).start()

    def finish(q):
        gather_copy(q, 0).wait_recv()
        for i in range(1, k_num):
            forward_copy(q, i).wait_recv()
        whole = w[q].astype(F32)
        for a in range(A_WIN):
            wa[q, a] = whole[:, a * c_loc : (a + 1) * c_loc, :].reshape(v, lc).astype(BF16)

    def turn(i):
        t_copy(i).wait()
        for j in range(0, v, 128):
            tf[j // 128] = traw[i % 2, :, :, pl.ds(j, 128)].astype(F32).reshape(pc * c_loc, 128)
        if i + 2 < t_num:
            t_copy(i + 2).start()
        phase, row = divmod(i * pc, ph_rows)
        for c in range(c_loc):
            for j in range(0, v, 128):
                tt[phase, c, pl.ds(row, pc), pl.ds(j, 128)] = tf[j // 128, pl.ds(c, pc, stride=c_loc), :].astype(BF16)

    def compute(phase, q):
        def step(g, _):
            first = pl.multiple_of(g * group, group)
            t = tt[phase, pl.ds(first, group)].reshape(group * ph_rows, v)
            for a in range(A_WIN):
                x = jnp.dot(t, wa[q, a], preferred_element_type=F32).astype(BF16)
                for j in range(group):
                    xbuf[pl.ds(a * ph_rows, ph_rows), pl.ds(j * lc, lc)] = x[j * ph_rows : (j + 1) * ph_rows]
            block = bv[pl.ds(first, group), pl.ds(q * lc, lc), :].reshape(group * lc, v)
            acc[...] += jnp.dot(xbuf[...], block, preferred_element_type=F32)
            return 0

        lax.fori_loop(0, c_loc // group, step, 0)

    def a_copy(phase):
        return remote(acct.at[phase, 1 - core], recv_a.at[phase], a_send.at[phase], a_recv.at[phase], sib)

    def b_copy(phase, i):
        to = lax.rem(chip + i, k_num)
        return remote(summed.at[phase, to], recv_b.at[phase, i - 1], b_send.at[phase, i], b_recv.at[phase, i], to * 2 + core)

    def scatter_pair(phase):
        turned = jnp.transpose(acc[...])
        for j in range(n):
            acct[phase, j % 2, j // 2] = turned[j * vb : (j + 1) * vb]
        a_copy(phase).start()

    def scatter_chips(phase):
        a_copy(phase).wait_recv()
        summed[phase] = acct[phase, core] + recv_a[phase]
        for i in range(1, k_num):
            b_copy(phase, i).start()

    def scatter_end(phase):
        total = summed[phase, chip]
        for i in range(1, k_num):
            b_copy(phase, i).wait_recv()
            total = total + recv_b[phase, i - 1]
        out[phase] = total

    for q in range(q_num):
        extract(q)
    for i in range(t_num):
        turn(i)
    forward(0)
    for phase in range(PHASES):
        acc[...] = jnp.zeros_like(acc)
        for q in range(q_num):
            if phase == 0:
                finish(q)
                if q + 1 < q_num:
                    forward(q + 1)
                rest_copy(q).wait()
            compute(phase, q)
            if phase > 0 and q == 0:
                scatter_chips(phase - 1)
        scatter_pair(phase)
    scatter_chips(PHASES - 1)
    for phase in range(PHASES):
        scatter_end(phase)

    for q in range(q_num):
        for i in range(k_num):
            gather_copy(q, i).wait_send()
        for i in range(1, k_num):
            forward_copy(q, i).wait_send()
    for phase in range(PHASES):
        a_copy(phase).wait_send()
        for i in range(1, k_num):
            b_copy(phase, i).wait_send()


def shards(n, cholesky, amplitudes):
    c_loc, nchol, v = cholesky.shape
    p_size = amplitudes.shape[0]
    lc = min(256, nchol)
    q_num = nchol // lc
    k_num = n // 2
    group = min(4, c_loc)
    pc = min(32, p_size // PHASES)
    ph_rows = p_size // PHASES
    vb = v // n
    rows = A_WIN * ph_rows
    dma = pltpu.SemaphoreType.DMA
    flops = 4 * A_WIN * p_size * c_loc * nchol * v
    res = pl.pallas_call(
        functools.partial(kernel, n, lc, group, pc),
        out_shape=jax.ShapeDtypeStruct((PHASES, vb, rows), F32),
        in_specs=[pl.BlockSpec(memory_space=pl.ANY)] * 2,
        out_specs=pl.BlockSpec(memory_space=pltpu.VMEM),
        scratch_shapes=[
            pltpu.VMEM((c_loc, nchol, v), BF16),
            pltpu.VMEM((PHASES, c_loc, ph_rows, v), BF16),
            pltpu.VMEM((2, pc, c_loc, v), BF16),
            pltpu.VMEM((v // 128, pc * c_loc, 128), F32),
            pltpu.VMEM((c_loc, 128, 128), BF16),
            pltpu.VMEM((q_num, n, A_WIN * c_loc, lc), BF16),
            pltpu.VMEM((q_num, A_WIN, v, lc), BF16),
            pltpu.VMEM((rows, group * lc), BF16),
            pltpu.VMEM((rows, v), F32),
            pltpu.VMEM((PHASES, 2, k_num, vb, rows), F32),
            pltpu.VMEM((PHASES, k_num, vb, rows), F32),
            pltpu.VMEM((PHASES, k_num, vb, rows), F32),
            pltpu.VMEM((PHASES, k_num - 1, vb, rows), F32),
            dma((q_num,)),
            dma((q_num,)),
            dma((2,)),
            dma((q_num, k_num)),
            dma((q_num, k_num)),
            dma((q_num, k_num)),
            dma((q_num, k_num)),
            dma((PHASES,)),
            dma((PHASES,)),
            dma((PHASES, k_num)),
            dma((PHASES, k_num)),
        ],
        compiler_params=pltpu.CompilerParams(
            collective_id=0, has_side_effects=True, vmem_limit_bytes=62 * 1024 * 1024),
        cost_estimate=pl.CostEstimate(flops=flops, bytes_accessed=2 * (cholesky.size + amplitudes.size), transcendentals=0),
    )(cholesky, amplitudes)
    res = res.reshape(PHASES, vb, A_WIN, ph_rows)
    return jnp.transpose(res, (0, 3, 2, 1)).reshape(p_size, A_WIN, vb)


def solution(mesh):
    in_specs = (P(("ga", "col"), None, None), P("ga", "col", None))
    out_specs = P("ga", None, "col")
    body = functools.partial(shards, mesh.shape["col"])
    return jax.shard_map(body, mesh=mesh, in_specs=in_specs, out_specs=out_specs, check_vma=False)
```

time: 195 us -> 86.6 us (0.44)
  waiting for transfers between devices: 101 us -> 0 us
  Pallas kernels: 0 us -> 84.8 us
  matrix products: 65.8 us -> 0 us
  between operations: 13.4 us -> 0.02 us
  local copies, waits for them, and re-layouts: 14.5 us -> 1.61 us
    pallas_call x0 -> x1, Pallas kernels: none -> 84.8 us  [shards(): pl.pallas_call(functools.partial(kernel, n, lc, group, pc), out_shape=jax...]
    dot_general x2 -> x0, matrix products: 65.8 us -> none  [the longest x1 43.2 us: shards(): jnp.einsum('clb,dal->acbd', cholesky, gathered, preferred_element_type=jn...]
    reduce_scatter x1 -> x0, waiting for transfers between devices: 56.3 us -> none  [shards(): lax.psum_scatter(partial_value, 'col', scatter_dimension=2, tiled=True)]
    all_gather x1 -> x0, waiting for transfers between devices: 44.2 us -> none  [shards(): gathered = lax.all_gather(window_local, 'col', axis=0, tiled=True)]
    slice x1 -> x0, local copies, waits for them, and re-layouts: 7.51 us -> none  [shards(): window_local = jnp.transpose(cholesky[:, :, :A_WIN], (0, 2, 1))]
    unnamed x1 -> x0, local copies, waits for them, and re-layouts: 6.97 us -> none
  transfers between devices with their start and end apart: 2 -> 0, of which waited for: 2 -> 0; matrix products, arithmetic and copies ran while one was open for 0% -> 0% of each run, Pallas kernels for 0% -> 0%
where the time goes in v1:
time: 86.6 us; the launch traced here: 86.4 us
  Pallas kernels  84.8 us (98%)
  local copies, waits for them, and re-layouts  1.61 us (2%)
    pallas_call x1, Pallas kernels, shards(): pl.pallas_call(functools.partial(kernel, n, lc, group, pc), out_shape=jax...  84.8 us

profile of v1, /device:TPU:0, one launch (start us, length us, event | category | flops | bytes accessed | tf_op | source)
XLA Modules:
  0.0 86.4 jit_solution(6061100351836504747)
XLA Ops:
  0.0 84.8 %shard_map.28 = f32[2,32,256]{2,1,0:T(8,128)} custom-call(bf16[32,1024,512]{2,1,0:T(8,128)(2,1)} %chol.1, bf16[256,32,512]{2,1,0:T(8,128)(2,1)} %amps.1), custom_call_target="tpu_custom_call" | custom-call | flops 34359738368 | bytes 41943040 | tf_op jit(solution)/shard_map/pallas_call | solution.py:204
  84.8 0.9 %reshape.6 = f32[2,32,2,128]{3,2,1,0:T(2,128)S(1)} reshape(f32[2,32,256]{2,1,0:T(8,128)} %shard_map.28) | data formatting | bytes 131072 | tf_op jit(solution)/shard_map/reshape | solution.py:239
  85.7 0.1 copy.3
  85.7 0.7 reshape.7

commit v2 on v1

--- a/solution.py
+++ b/solution.py
@@ -35,17 +35,17 @@
         return lax.rem(chip - i + k_num, k_num) * 2 + core
 
     def lane_copy(q):
-        rows = pl.ds(q * lc, lc)
+        rows = pl.ds(pl.multiple_of(q * lc, lc), lc)
         return pltpu.make_async_copy(chol.at[:, rows, pl.ds(0, 128)], bv.at[:, rows, pl.ds(0, 128)], lane_sem.at[q])
 
     def rest_copy(q):
-        rows = pl.ds(q * lc, lc)
+        rows = pl.ds(pl.multiple_of(q * lc, lc), lc)
         return pltpu.make_async_copy(chol.at[:, rows, pl.ds(128, v - 128)], bv.at[:, rows, pl.ds(128, v - 128)], rest_sem.at[q])
 
     t_num = p_size // pc
 
     def t_copy(i):
-        return pltpu.make_async_copy(amps.at[pl.ds(i * pc, pc)], traw.at[i % 2], t_sem.at[i % 2])
+        return pltpu.make_async_copy(amps.at[pl.ds(i * pc, pc)], traw.at[lax.rem(i, 2)], t_sem.at[lax.rem(i, 2)])
 
     for q in range(q_num):
         lane_copy(q).start()
@@ -85,7 +85,7 @@
         lane_copy(q).wait()
 
         def step(c, z):
-            return z + jnp.dot(bv[c, pl.ds(q * lc, lc), pl.ds(0, 128)], sel[c], preferred_element_type=F32)
+            return z + jnp.dot(bv[c, pl.ds(pl.multiple_of(q * lc, lc), lc), pl.ds(0, 128)], sel[c], preferred_element_type=F32)
 
         z = lax.fori_loop(0, c_loc, step, jnp.zeros((lc, 128), F32), unroll=4)
         w[q, me] = jnp.transpose(z)[: A_WIN * c_loc].astype(BF16)
@@ -108,10 +108,14 @@
     def turn(i):
         t_copy(i).wait()
         for j in range(0, v, 128):
-            tf[j // 128] = traw[i % 2, :, :, pl.ds(j, 128)].astype(F32).reshape(pc * c_loc, 128)
-        if i + 2 < t_num:
+            tf[j // 128] = traw[lax.rem(i, 2), :, :, pl.ds(j, 128)].astype(F32).reshape(pc * c_loc, 128)
+
+        @pl.when(i + 2 < t_num)
+        def _():
             t_copy(i + 2).start()
-        phase, row = divmod(i * pc, ph_rows)
+
+        phase = i * pc // ph_rows
+        row = pl.multiple_of(lax.rem(i * pc, ph_rows), pc)
         for c in range(c_loc):
             for j in range(0, v, 128):
                 tt[phase, c, pl.ds(row, pc), pl.ds(j, 128)] = tf[j // 128, pl.ds(c, pc, stride=c_loc), :].astype(BF16)
@@ -124,11 +128,11 @@
                 x = jnp.dot(t, wa[q, a], preferred_element_type=F32).astype(BF16)
                 for j in range(group):
                     xbuf[pl.ds(a * ph_rows, ph_rows), pl.ds(j * lc, lc)] = x[j * ph_rows : (j + 1) * ph_rows]
-            block = bv[pl.ds(first, group), pl.ds(q * lc, lc), :].reshape(group * lc, v)
+            block = bv[pl.ds(first, group), pl.ds(pl.multiple_of(q * lc, lc), lc), :].reshape(group * lc, v)
             acc[...] += jnp.dot(xbuf[...], block, preferred_element_type=F32)
             return 0
 
-        lax.fori_loop(0, c_loc // group, step, 0)
+        lax.fori_loop(0, c_loc // group, step, 0, unroll=2)
 
     def a_copy(phase):
         return remote(acct.at[phase, 1 - core], recv_a.at[phase], a_send.at[phase], a_recv.at[phase], sib)
@@ -156,23 +160,45 @@
             total = total + recv_b[phase, i - 1]
         out[phase] = total
 
-    for q in range(q_num):
-        extract(q)
-    for i in range(t_num):
-        turn(i)
+    def loop(count, body):
+        def step(i, _):
+            body(i)
+            return 0
+
+        lax.fori_loop(0, count, step, 0)
+
+    loop(q_num, extract)
+    loop(t_num, turn)
     forward(0)
-    for phase in range(PHASES):
-        acc[...] = jnp.zeros_like(acc)
-        for q in range(q_num):
-            if phase == 0:
-                finish(q)
-                if q + 1 < q_num:
-                    forward(q + 1)
-                rest_copy(q).wait()
-            compute(phase, q)
-            if phase > 0 and q == 0:
-                scatter_chips(phase - 1)
-        scatter_pair(phase)
+
+    def chunk(i):
+        phase, q = i // q_num, lax.rem(i, q_num)
+
+        @pl.when(q == 0)
+        def _():
+            acc[...] = jnp.zeros_like(acc)
+
+        @pl.when(phase == 0)
+        def _():
+            finish(q)
+
+            @pl.when(q + 1 < q_num)
+            def _():
+                forward(q + 1)
+
+            rest_copy(q).wait()
+
+        compute(phase, q)
+
+        @pl.when((phase > 0) & (q == 0))
+        def _():
+            scatter_chips(phase - 1)
+
+        @pl.when(q == q_num - 1)
+        def _():
+            scatter_pair(phase)
+
+    loop(PHASES * q_num, chunk)
     scatter_chips(PHASES - 1)
     for phase in range(PHASES):
         scatter_end(phase)

time: 86.6 us -> 81.3 us (0.939)
  Pallas kernels: 84.8 us -> 79.5 us
    pallas_call x1, Pallas kernels: 84.8 us -> 79.5 us  [shards(): pl.pallas_call(functools.partial(kernel, n, lc, group, pc), out_shape=jax...]
where the time goes in v2:
time: 81.3 us; the launch traced here: 81.1 us
  Pallas kernels  79.5 us (98%)
  local copies, waits for them, and re-layouts  1.61 us (2%)
    pallas_call x1, Pallas kernels, shards(): pl.pallas_call(functools.partial(kernel, n, lc, group, pc), out_shape=jax...  79.5 us

profile of v2, /device:TPU:0, one launch (start us, length us, event | category | flops | bytes accessed | tf_op | source)
XLA Modules:
  0.0 81.1 jit_solution(3098723871029728100)
XLA Ops:
  0.0 79.5 %shard_map.28 = f32[2,32,256]{2,1,0:T(8,128)} custom-call(bf16[32,1024,512]{2,1,0:T(8,128)(2,1)} %chol.1, bf16[256,32,512]{2,1,0:T(8,128)(2,1)} %amps.1), custom_call_target="tpu_custom_call" | custom-call | flops 34359738368 | bytes 41943040 | tf_op jit(solution)/shard_map/pallas_call | solution.py:230
  79.5 0.9 %reshape.6 = f32[2,32,2,128]{3,2,1,0:T(2,128)S(1)} reshape(f32[2,32,256]{2,1,0:T(8,128)} %shard_map.28) | data formatting | bytes 131072 | tf_op jit(solution)/shard_map/reshape | solution.py:265
  80.4 0.1 copy.3
  80.4 0.7 reshape.7
